TPU v7x, 32 devices: a whole 2x2x4 slice. The times are simulated.
32 devices in a mesh: ctx: 16 (over z, y, x), fsdp: 2 (over core).
Axes of the slice: x: 2, y: 2, z: 4, core: 2. Of those that a mesh axis runs over, the one named last changes fastest.
Arguments:
- x_in: bfloat16 [4, 1024, 576], P('fsdp', 'ctx')
- w_query: bfloat16 [576, 576], P('fsdp'), may hold values from -0.25 to 0.25
- w_key: bfloat16 [576, 192], P('fsdp'), may hold values from -0.25 to 0.25
- w_value: bfloat16 [576, 192], P('fsdp'), may hold values from -0.25 to 0.25
- w_out: bfloat16 [576, 576], P('fsdp'), may hold values from -6 to 6
- attn_gain: bfloat16 [576], P('fsdp'), may hold values from 0.5 to 1.5
- w_gate: bfloat16 [576, 1536], P('fsdp'), may hold values from -0.25 to 0.25
- w_up: bfloat16 [576, 1536], P('fsdp'), may hold values from -0.25 to 0.25
- w_down: bfloat16 [1536, 576], P('fsdp'), may hold values from -0.15625 to 0.15625
- mlp_gain: bfloat16 [576], P('fsdp'), may hold values from 0.5 to 1.5
- block_of_slot: int32 [32], replicated, may hold values from 0 to 31, as said below
- out_grad: bfloat16 [4, 1024, 576], P('fsdp', 'ctx'), may hold values from -6 to 6
Outputs:
- y_out: bfloat16 [4, 1024, 576], P('fsdp', 'ctx')
- x_grad: bfloat16 [4, 1024, 576], P('fsdp', 'ctx')
- grad_w_query: float32 [576, 576], P('fsdp')
- grad_w_key: float32 [576, 192], P('fsdp')
- grad_w_value: float32 [576, 192], P('fsdp')
- grad_w_out: float32 [576, 576], P('fsdp')
- grad_attn_gain: float32 [576], P('fsdp')
- grad_w_gate: float32 [576, 1536], P('fsdp')
- grad_w_up: float32 [576, 1536], P('fsdp')
- grad_w_down: float32 [1536, 576], P('fsdp')
- grad_mlp_gain: float32 [576], P('fsdp')
Inputs may be any that keep to these rules, and one draw needn't show every extreme that they name: `block_of_slot`: the entries are a permutation of 0 to 31 and entries 2 i and 2 i + 1 sum to 31, so slots 2 i and 2 i + 1 hold a block from the front of the sequence and its mirror from the back.
All inputs are finite; a program needn't handle non-finite values.
Results may differ from a plain program's by a relative error of at most 0.025.
Values may be sent and summed in bfloat16 or wider, within the bound.
A program may use at most 128 MiB of HBM per device.

v0:
```python
import jax
import jax.numpy as jnp
from jax import lax
from jax.sharding import PartitionSpec as P

HEADS = 9
KV_HEADS = 3
HEAD_DIM = 64
epsilon = 1e-05
theta_base = 100000.0
masked_value = -1e30


def shifted(block, axis, distance):
    devices = range(lax.axis_size(axis))
    route = [((i - distance) % len(devices), i) for i in devices]
    return lax.ppermute(block, axis, route)


def make_tables(positions):
    half_dim = HEAD_DIM // 2
    frequency = theta_base ** (-2.0 * jnp.arange(half_dim, dtype=jnp.float32) / HEAD_DIM)
    angles = positions.astype(jnp.float32)[:, None] * frequency[None, :]
    return (jnp.cos(angles), jnp.sin(angles))


def rotate(values, cosine, sine):
    half_dim = values.shape[-1] // 2
    first_half = values[..., :half_dim]
    second_half = values[..., half_dim:]
    cos_rows = cosine[:, None, :]
    sin_rows = sine[:, None, :]
    return jnp.concatenate(
        [
            first_half * cos_rows - second_half * sin_rows,
            second_half * cos_rows + first_half * sin_rows,
        ],
        axis=-1,
    )


def rotate_back(grads, cosine, sine):
    half_dim = grads.shape[-1] // 2
    first_half = grads[..., :half_dim]
    second_half = grads[..., half_dim:]
    cos_rows = cosine[:, None, :]
    sin_rows = sine[:, None, :]
    return jnp.concatenate(
        [
            first_half * cos_rows + second_half * sin_rows,
            second_half * cos_rows - first_half * sin_rows,
        ],
        axis=-1,
    )


def slot_positions(block_of_slot, offset, count_rows, half_len):
    row_ids = offset + jnp.arange(count_rows, dtype=jnp.int32)
    slot_ids = row_ids // half_len
    slot_match = slot_ids[:, None] == jnp.arange(block_of_slot.shape[0], dtype=jnp.int32)[None, :]
    owners = jnp.sum(jnp.where(slot_match, block_of_slot[None, :], 0), axis=1)
    return owners * half_len + row_ids % half_len


def norm_forward(values, gain_vec):
    inverse = lax.rsqrt(jnp.mean(values * values, axis=-1, keepdims=True) + epsilon)
    scaled = values * inverse
    return (scaled * gain_vec, scaled, inverse)


def norm_backward(grad_output, gain_vec, scaled, inverse):
    grad_scaled = grad_output * gain_vec
    grad_input = inverse * (
        grad_scaled - scaled * jnp.mean(grad_scaled * scaled, axis=-1, keepdims=True)
    )
    grad_gain = jnp.sum(grad_output * scaled, axis=0)
    return (grad_input, grad_gain)


def local(
    x_in,
    w_query,
    w_key,
    w_value,
    w_out,
    attn_gain,
    w_gate,
    w_up,
    w_down,
    mlp_gain,
    block_of_slot,
    out_grad,
):
    gathered = (
        lax.all_gather(w_query, "fsdp", axis=0, tiled=True),
        lax.all_gather(w_key, "fsdp", axis=0, tiled=True),
        lax.all_gather(w_value, "fsdp", axis=0, tiled=True),
        lax.all_gather(w_out, "fsdp", axis=0, tiled=True),
        lax.all_gather(attn_gain, "fsdp", axis=0, tiled=True),
        lax.all_gather(w_gate, "fsdp", axis=0, tiled=True),
        lax.all_gather(w_up, "fsdp", axis=0, tiled=True),
        lax.all_gather(w_down, "fsdp", axis=0, tiled=True),
        lax.all_gather(mlp_gain, "fsdp", axis=0, tiled=True),
    )
    (
        full_query,
        full_key,
        full_value,
        full_out,
        gain_attn,
        full_gate,
        full_up,
        full_down,
        gain_mlp,
    ) = gathered
    gain_attn_f = gain_attn.astype(jnp.float32)
    gain_mlp_f = gain_mlp.astype(jnp.float32)
    seq_count, tok_count, model_width = x_in.shape
    group_size = HEADS // KV_HEADS
    half_len = tok_count // 2
    rows_all = seq_count * tok_count
    ctx_count = lax.axis_size("ctx")
    score_scale = HEAD_DIM ** (-0.5)
    my_offset = lax.axis_index("ctx") * tok_count
    query_pos = slot_positions(block_of_slot, my_offset, tok_count, half_len)
    cosine, sine = make_tables(query_pos)
    inputs = x_in.astype(jnp.float32).reshape(rows_all, model_width)
    normed_f, scaled_one, inverse_one = norm_forward(inputs, gain_attn_f)
    normed = normed_f.astype(jnp.bfloat16)
    query_f = jnp.dot(normed, full_query, preferred_element_type=jnp.float32).reshape(
        seq_count, tok_count, HEADS, HEAD_DIM
    )
    queries = (
        rotate(query_f, cosine, sine)
        .astype(jnp.bfloat16)
        .reshape(seq_count, tok_count, KV_HEADS, group_size, HEAD_DIM)
    )
    key_f = jnp.dot(normed, full_key, preferred_element_type=jnp.float32).reshape(
        seq_count, tok_count, KV_HEADS, HEAD_DIM
    )
    key_rows = rotate(key_f, cosine, sine).astype(jnp.bfloat16)
    value_rows = (
        jnp.dot(normed, full_value, preferred_element_type=jnp.float32)
        .astype(jnp.bfloat16)
        .reshape(seq_count, tok_count, KV_HEADS, HEAD_DIM)
    )
    stat_shape = (seq_count, KV_HEADS, group_size, tok_count)
    running_max = jnp.full(stat_shape, masked_value, jnp.float32)
    key_part = lax.all_gather(key_rows, "ctx", axis=1, tiled=True)
    value_part = lax.all_gather(value_rows, "ctx", axis=1, tiled=True)
    key_pos = slot_positions(block_of_slot, jnp.int32(0), key_part.shape[1], half_len)
    visible = query_pos[:, None] >= key_pos[None, :]
    scores = (
        jnp.einsum("sqkgd,snkd->skgqn", queries, key_part, preferred_element_type=jnp.float32)
        * score_scale
    )
    scores = jnp.where(visible, scores, masked_value)
    new_max = jnp.maximum(running_max, jnp.max(scores, axis=-1))
    weights = jnp.where(visible, jnp.exp(scores - new_max[..., None]), 0.0)
    totals = jnp.sum(weights, axis=-1)
    weighted_sum = jnp.einsum(
        "skgqn,snkd->skgqd",
        weights.astype(jnp.bfloat16),
        value_part,
        preferred_element_type=jnp.float32,
    )
    running_max, totals, weighted_sum = (new_max, totals, weighted_sum)
    log_total = running_max + jnp.log(totals)
    attended_f = weighted_sum / totals[..., None]
    attended = (
        attended_f.transpose(0, 3, 1, 2, 4).reshape(rows_all, model_width).astype(jnp.bfloat16)
    )
    hidden_state = inputs + jnp.dot(attended, full_out, preferred_element_type=jnp.float32)
    normed_two_f, scaled_two, inverse_two = norm_forward(hidden_state, gain_mlp_f)
    normed_two = normed_two_f.astype(jnp.bfloat16)
    gate_vals = jnp.dot(normed_two, full_gate, preferred_element_type=jnp.float32)
    up_vals = jnp.dot(normed_two, full_up, preferred_element_type=jnp.float32)
    sigmoid_gate = jax.nn.sigmoid(gate_vals)
    activated = gate_vals * sigmoid_gate
    inner_rows = (activated * up_vals).astype(jnp.bfloat16)
    result = hidden_state + jnp.dot(inner_rows, full_down, preferred_element_type=jnp.float32)
    y_out = result.reshape(seq_count, tok_count, model_width).astype(jnp.bfloat16)
    grad_top = out_grad.reshape(rows_all, model_width)
    grad_residual = grad_top.astype(jnp.float32)
    grad_wdown = jnp.einsum("rf,rd->fd", inner_rows, grad_top, preferred_element_type=jnp.float32)
    grad_inner = jnp.einsum("rd,fd->rf", grad_top, full_down, preferred_element_type=jnp.float32)
    grad_gate = (
        grad_inner * up_vals * sigmoid_gate * (1.0 + gate_vals * (1.0 - sigmoid_gate))
    ).astype(jnp.bfloat16)
    grad_up = (grad_inner * activated).astype(jnp.bfloat16)
    grad_wgate = jnp.einsum("rd,rf->df", normed_two, grad_gate, preferred_element_type=jnp.float32)
    grad_wup = jnp.einsum("rd,rf->df", normed_two, grad_up, preferred_element_type=jnp.float32)
    grad_normed_two = jnp.einsum(
        "rf,df->rd", grad_gate, full_gate, preferred_element_type=jnp.float32
    ) + jnp.einsum("rf,df->rd", grad_up, full_up, preferred_element_type=jnp.float32)
    grad_hidden_norm, grad_gain_mlp = norm_backward(
        grad_normed_two, gain_mlp_f, scaled_two, inverse_two
    )
    grad_hidden = grad_residual + grad_hidden_norm
    grad_branch = grad_hidden.astype(jnp.bfloat16)
    grad_wout = jnp.einsum("ri,rj->ij", attended, grad_branch, preferred_element_type=jnp.float32)
    grad_attended = jnp.einsum(
        "rj,ij->ri", grad_branch, full_out, preferred_element_type=jnp.float32
    ).astype(jnp.bfloat16)
    grad_heads = grad_attended.reshape(
        seq_count, tok_count, KV_HEADS, group_size, HEAD_DIM
    ).transpose(0, 2, 3, 1, 4)
    row_delta = jnp.sum(grad_heads.astype(jnp.float32) * attended_f, axis=-1)

    def block_grads(key_part, value_part, offset):
        key_pos = slot_positions(block_of_slot, offset, key_part.shape[1], half_len)
        visible = query_pos[:, None] >= key_pos[None, :]
        scores = (
            jnp.einsum("sqkgd,snkd->skgqn", queries, key_part, preferred_element_type=jnp.float32)
            * score_scale
        )
        weights = jnp.where(visible, jnp.exp(scores - log_total[..., None]), 0.0)
        grad_value_part = jnp.einsum(
            "skgqn,skgqd->snkd",
            weights.astype(jnp.bfloat16),
            grad_heads,
            preferred_element_type=jnp.float32,
        )
        grad_weights = jnp.einsum(
            "skgqd,snkd->skgqn", grad_heads, value_part, preferred_element_type=jnp.float32
        )
        grad_scores = (weights * (grad_weights - row_delta[..., None])).astype(jnp.bfloat16)
        grad_query_part = jnp.einsum(
            "skgqn,snkd->skgqd", grad_scores, key_part, preferred_element_type=jnp.float32
        )
        grad_key_part = (
            jnp.einsum(
                "skgqn,sqkgd->snkd", grad_scores, queries, preferred_element_type=jnp.float32
            )
            * score_scale
        )
        return (grad_query_part, grad_key_part, grad_value_part)

    grad_query_init = jnp.zeros(stat_shape + (HEAD_DIM,), jnp.float32)
    kv_zero = jnp.zeros(key_rows.shape, jnp.float32)

    def one_hop(hop_index, loop_state):
        key_part, value_part, grad_query, grad_key, grad_value = loop_state
        source = (lax.axis_index("ctx") - hop_index) % ctx_count
        grad_query_part, grad_key_part, grad_value_part = block_grads(
            key_part, value_part, source * tok_count
        )
        key_part, value_part = shifted((key_part, value_part), "ctx", 1)
        grad_key, grad_value = (
            shifted((grad_key + grad_key_part).astype(jnp.bfloat16), "ctx", 1).astype(jnp.float32),
            shifted((grad_value + grad_value_part).astype(jnp.bfloat16), "ctx", 1).astype(
                jnp.float32
            ),
        )
        return (key_part, value_part, grad_query + grad_query_part, grad_key, grad_value)

    loop_state = lax.fori_loop(
        0, ctx_count - 1, one_hop, (key_rows, value_rows, grad_query_init, kv_zero, kv_zero)
    )
    key_part, value_part, grad_query, grad_key, grad_value = loop_state
    source = (lax.axis_index("ctx") + 1) % ctx_count
    grad_query_part, grad_key_part, grad_value_part = block_grads(
        key_part, value_part, source * tok_count
    )
    grad_query = grad_query + grad_query_part
    grad_key, grad_value = (
        shifted((grad_key + grad_key_part).astype(jnp.bfloat16), "ctx", 1).astype(jnp.float32),
        shifted((grad_value + grad_value_part).astype(jnp.bfloat16), "ctx", 1).astype(jnp.float32),
    )
    grad_query_rows = (
        (grad_query * score_scale)
        .transpose(0, 3, 1, 2, 4)
        .reshape(seq_count, tok_count, HEADS, HEAD_DIM)
    )
    grad_query_low = (
        rotate_back(grad_query_rows, cosine, sine)
        .astype(jnp.bfloat16)
        .reshape(rows_all, model_width)
    )
    grad_key_low = (
        rotate_back(grad_key, cosine, sine)
        .astype(jnp.bfloat16)
        .reshape(rows_all, KV_HEADS * HEAD_DIM)
    )
    grad_value_low = grad_value.astype(jnp.bfloat16).reshape(rows_all, KV_HEADS * HEAD_DIM)
    grad_wquery = jnp.einsum(
        "rd,re->de", normed, grad_query_low, preferred_element_type=jnp.float32
    )
    grad_wkey = jnp.einsum("rd,re->de", normed, grad_key_low, preferred_element_type=jnp.float32)
    grad_wvalue = jnp.einsum(
        "rd,re->de", normed, grad_value_low, preferred_element_type=jnp.float32
    )
    grad_normed = jnp.einsum(
        "re,de->rd", grad_query_low, full_query, preferred_element_type=jnp.float32
    )
    grad_normed = grad_normed + jnp.einsum(
        "re,de->rd", grad_key_low, full_key, preferred_element_type=jnp.float32
    )
    grad_normed = grad_normed + jnp.einsum(
        "re,de->rd", grad_value_low, full_value, preferred_element_type=jnp.float32
    )
    grad_input_norm, grad_gain_attn = norm_backward(
        grad_normed, gain_attn_f, scaled_one, inverse_one
    )
    x_grad = (
        (grad_hidden + grad_input_norm)
        .astype(jnp.bfloat16)
        .reshape(seq_count, tok_count, model_width)
    )
    owned_grads = (
        lax.psum_scatter(
            grad_wquery.astype(jnp.bfloat16), "fsdp", scatter_dimension=0, tiled=True
        ).astype(jnp.float32),
        lax.psum_scatter(
            grad_wkey.astype(jnp.bfloat16), "fsdp", scatter_dimension=0, tiled=True
        ).astype(jnp.float32),
        lax.psum_scatter(
            grad_wvalue.astype(jnp.bfloat16), "fsdp", scatter_dimension=0, tiled=True
        ).astype(jnp.float32),
        lax.psum_scatter(
            grad_wout.astype(jnp.bfloat16), "fsdp", scatter_dimension=0, tiled=True
        ).astype(jnp.float32),
        lax.psum_scatter(
            grad_gain_attn.astype(jnp.bfloat16), "fsdp", scatter_dimension=0, tiled=True
        ).astype(jnp.float32),
        lax.psum_scatter(
            grad_wgate.astype(jnp.bfloat16), "fsdp", scatter_dimension=0, tiled=True
        ).astype(jnp.float32),
        lax.psum_scatter(
            grad_wup.astype(jnp.bfloat16), "fsdp", scatter_dimension=0, tiled=True
        ).astype(jnp.float32),
        lax.psum_scatter(
            grad_wdown.astype(jnp.bfloat16), "fsdp", scatter_dimension=0, tiled=True
        ).astype(jnp.float32),
        lax.psum_scatter(
            grad_gain_mlp.astype(jnp.bfloat16), "fsdp", scatter_dimension=0, tiled=True
        ).astype(jnp.float32),
    )
    summed_grads = (
        lax.psum(owned_grads[0].astype(jnp.bfloat16), "ctx").astype(jnp.float32),
        lax.psum(owned_grads[1].astype(jnp.bfloat16), "ctx").astype(jnp.float32),
        lax.psum(owned_grads[2].astype(jnp.bfloat16), "ctx").astype(jnp.float32),
        lax.psum(owned_grads[3].astype(jnp.bfloat16), "ctx").astype(jnp.float32),
        lax.psum(owned_grads[4].astype(jnp.bfloat16), "ctx").astype(jnp.float32),
        lax.psum(owned_grads[5].astype(jnp.bfloat16), "ctx").astype(jnp.float32),
        lax.psum(owned_grads[6].astype(jnp.bfloat16), "ctx").astype(jnp.float32),
        lax.psum(owned_grads[7].astype(jnp.bfloat16), "ctx").astype(jnp.float32),
        lax.psum(owned_grads[8].astype(jnp.bfloat16), "ctx").astype(jnp.float32),
    )
    return (
        y_out,
        x_grad,
        summed_grads[0],
        summed_grads[1],
        summed_grads[2],
        summed_grads[3],
        summed_grads[4],
        summed_grads[5],
        summed_grads[6],
        summed_grads[7],
        summed_grads[8],
    )


def solution(mesh):
    placed = (
        P("fsdp", "ctx", None),
        P("fsdp", None),
        P("fsdp", None),
        P("fsdp", None),
        P("fsdp", None),
        P("fsdp"),
        P("fsdp", None),
        P("fsdp", None),
        P("fsdp", None),
        P("fsdp"),
        P(),
        P("fsdp", "ctx", None),
    )
    return jax.shard_map(
        local,
        mesh=mesh,
        in_specs=placed,
        out_specs=(
            P("fsdp", "ctx", None),
            P("fsdp", "ctx", None),
            P("fsdp", None),
            P("fsdp", None),
            P("fsdp", None),
            P("fsdp", None),
            P("fsdp"),
            P("fsdp", None),
            P("fsdp", None),
            P("fsdp", None),
            P("fsdp"),
        ),
        check_vma=False,
    )
```

profile of v0, /device:TPU:0, one launch (start us, length us, event | category | flops | bytes accessed | tf_op | source)
XLA Modules:
  0.0 655.3 jit_solution(17104645423890764450)
XLA Ops:
  18.4 54.9 %all_gather.35 = bf16[2,1024,3,64]{3,0,2,1:T(2,128)(2,1)} all-gather(bf16[2,64,3,64]{3,0,2,1:T(2,128)(2,1)S(1)} %copy.115), channel_id=1, replica_groups=mesh['ctx'=16,'fsdp'=2] {'ctx'}, dimensions={1}, use_global_device_ids=true | all-gather | bytes 835584 | tf_op jit(solution)/shard_map/all_gather | solution.py:149
  84.5 49.6 %all_gather.38 = bf16[2,1024,3,64]{3,0,2,1:T(2,128)(2,1)S(1)} all-gather(bf16[2,64,3,64]{3,0,2,1:T(2,128)(2,1)S(1)} %copy.121), channel_id=1, replica_groups=mesh['ctx'=16,'fsdp'=2] {'ctx'}, dimensions={1}, use_global_device_ids=true | all-gather | bytes 835584 | tf_op jit(solution)/shard_map/all_gather | solution.py:150
  134.2 3.9 fusion.18
  154.5 3.5 multiply_convert_fusion
  163.3 216.1 %while.25 = (s32[]{:T(128)}, bf16[2,64,3,64]{3,1,2,0:T(8,128)(2,1)S(1)}, bf16[2,64,3,64]{3,1,2,0:T(8,128)(2,1)S(1)}, f32[2,3,3,64,64]{4,3,2,1,0:T(8,128)S(1)}, f...) while((s32[]{:T(128)}, ...), condition=%wide.region_10.11_spmd.clone, body=%wide.region_8.10_spmd.clone.sunk | while | flops 48082768 | bytes 4246918 | solution.py:257
  168.7 8.0 %collective-permute-done.2 = bf16[2,64,3,64]{3,1,2,0:T(8,128)(2,1)S(1)} collective-permute-done((bf16[2,64,3,64]{3,1,2,0:T(8,128)(2,1)S(1)}, bf16[2,64,3,64]{3,1,2,0:T(8,128)(2,1)S(1)}, u32[]{:S(2)}, u32[]{:S(2)}) %collective-permute-start.2) | collective-permute-done | bytes 49184 | tf_op jit(solution)/shard_map/while/body/eval_jaxpr/ppermute | solution.py:17
  182.3 8.6 %collective-permute-done.2 = bf16[2,64,3,64]{3,1,2,0:T(8,128)(2,1)S(1)} collective-permute-done((bf16[2,64,3,64]{3,1,2,0:T(8,128)(2,1)S(1)}, bf16[2,64,3,64]{3,1,2,0:T(8,128)(2,1)S(1)}, u32[]{:S(2)}, u32[]{:S(2)}) %collective-permute-start.2) | collective-permute-done | bytes 49184 | tf_op jit(solution)/shard_map/while/body/eval_jaxpr/ppermute | solution.py:17
  199.3 5.9 collective-permute-done.2
  214.3 5.3 collective-permute-done.2
  228.3 5.3 collective-permute-done.2
  238.9 4.3 collective-permute-start.3
  243.6 3.4 collective-permute-done.2
  248.3 3.4 collective-permute-start.1
  258.3 4.9 collective-permute-done.2
  271.3 5.8 collective-permute-done.2
  285.5 6.4 collective-permute-done.2
  297.7 3.1 collective-permute-start.3
  301.2 6.1 collective-permute-done.2
  314.8 8.1 %collective-permute-done.2 = bf16[2,64,3,64]{3,1,2,0:T(8,128)(2,1)S(1)} collective-permute-done((bf16[2,64,3,64]{3,1,2,0:T(8,128)(2,1)S(1)}, bf16[2,64,3,64]{3,1,2,0:T(8,128)(2,1)S(1)}, u32[]{:S(2)}, u32[]{:S(2)}) %collective-permute-start.2) | collective-permute-done | bytes 49184 | tf_op jit(solution)/shard_map/while/body/eval_jaxpr/ppermute | solution.py:17
  328.5 8.6 %collective-permute-done.2 = bf16[2,64,3,64]{3,1,2,0:T(8,128)(2,1)S(1)} collective-permute-done((bf16[2,64,3,64]{3,1,2,0:T(8,128)(2,1)S(1)}, bf16[2,64,3,64]{3,1,2,0:T(8,128)(2,1)S(1)}, u32[]{:S(2)}, u32[]{:S(2)}) %collective-permute-start.2) | collective-permute-done | bytes 49184 | tf_op jit(solution)/shard_map/while/body/eval_jaxpr/ppermute | solution.py:17
  344.6 6.6 %collective-permute-done.2 = bf16[2,64,3,64]{3,1,2,0:T(8,128)(2,1)S(1)} collective-permute-done((bf16[2,64,3,64]{3,1,2,0:T(8,128)(2,1)S(1)}, bf16[2,64,3,64]{3,1,2,0:T(8,128)(2,1)S(1)}, u32[]{:S(2)}, u32[]{:S(2)}) %collective-permute-start.2) | collective-permute-done | bytes 49184 | tf_op jit(solution)/shard_map/while/body/eval_jaxpr/ppermute | solution.py:17
  357.6 7.6 %collective-permute-done.2 = bf16[2,64,3,64]{3,1,2,0:T(8,128)(2,1)S(1)} collective-permute-done((bf16[2,64,3,64]{3,1,2,0:T(8,128)(2,1)S(1)}, bf16[2,64,3,64]{3,1,2,0:T(8,128)(2,1)S(1)}, u32[]{:S(2)}, u32[]{:S(2)}) %collective-permute-start.2) | collective-permute-done | bytes 49184 | tf_op jit(solution)/shard_map/while/body/eval_jaxpr/ppermute | solution.py:17
  373.3 5.0 collective-permute-done.2
  381.8 7.3 %collective-permute-done.5 = bf16[2,64,3,64]{1,3,2,0:T(8,128)(2,1)S(1)} collective-permute-done((bf16[2,64,3,64]{1,3,2,0:T(8,128)(2,1)S(1)}, bf16[2,64,3,64]{1,3,2,0:T(8,128)(2,1)S(1)}, u32[]{:S(2)}, u32[]{:S(2)}) %collective-permute-start.5) | collective-permute-done | bytes 49184 | tf_op jit(solution)/shard_map/ppermute | solution.py:17
  401.6 3.7 reduce-scatter.10.cloned.1.call-done
  405.3 11.5 %reduce-scatter.14.cloned.1.call-done = bf16[288,576]{1,0:T(8,128)(2,1)} async-done(((bf16[576,576]{1,0:T(8,128)(2,1)}), bf16[288,576]{1,0:T(8,128)(2,1)}) %reduce-scatter.14.cloned.1.call-update) | async-done | bytes 331792 | tf_op jit(solution)/shard_map/reduce_scatter | solution.py:320
  416.8 12.2 %reduce-scatter.8.cloned.1.call-done = bf16[288,576]{1,0:T(8,128)(2,1)} async-done(((bf16[576,576]{1,0:T(8,128)(2,1)}), bf16[288,576]{1,0:T(8,128)(2,1)}) %reduce-scatter.8.cloned.1.call-update) | async-done | bytes 331792 | tf_op jit(solution)/shard_map/reduce_scatter | solution.py:311
  429.0 13.3 %reduce-scatter.18.cloned.1.call-done = bf16[288,1536]{1,0:T(8,128)(2,1)} async-done(((bf16[576,1536]{1,0:T(8,128)(2,1)}), bf16[288,1536]{1,0:T(8,128)(2,1)}) %reduce-scatter.18.cloned.1.call-update) | async-done | bytes 884752 | tf_op jit(solution)/shard_map/reduce_scatter | solution.py:329
  442.4 13.4 %reduce-scatter.16.cloned.1.call-done = bf16[288,1536]{1,0:T(8,128)(2,1)} async-done(((bf16[576,1536]{1,0:T(8,128)(2,1)}), bf16[288,1536]{1,0:T(8,128)(2,1)}) %reduce-scatter.16.cloned.1.call-update) | async-done | bytes 884752 | tf_op jit(solution)/shard_map/reduce_scatter | solution.py:326
  455.8 13.2 %reduce-scatter.20.cloned.1.call-done = bf16[768,576]{0,1:T(8,128)(2,1)} async-done(((bf16[1536,576]{0,1:T(8,128)(2,1)}), bf16[768,576]{0,1:T(8,128)(2,1)}) %reduce-scatter.20.cloned.1.call-update) | async-done | bytes 884752 | tf_op jit(solution)/shard_map/reduce_scatter | solution.py:332
  476.4 43.7 %all-reduce.4 = (bf16[288]{0:T(512)(128)(2,1)S(1)}, bf16[288]{0:T(512)(128)(2,1)S(1)}) all-reduce(bf16[288]{0:T(512)(128)(2,1)S(1)} %dynamic-slice.3, bf16[288]{0:T(512)(128)(2,1)S(1)} %dynamic-slice.5), channel_id=1, replica_groups=mesh['ctx'=16,'fsdp'=2] {'ctx'}, use_global_device_ids=true, to_apply=%region_23.24 | all-reduce | flops 576 | bytes 2304 | tf_op jit(solution)/shard_map/psum | solution.py:344
  522.2 117.8 %all-reduce.10.cloned.1.call-done = (bf16[288,576]{1,0:T(8,128)(2,1)}, bf16[288,192]{1,0:T(8,128)(2,1)}, bf16[288,192]{1,0:T(8,128)(2,1)}, bf16[288,576]{1,0:T(8...) async-done(((bf16[288,576]{1,0:T(8,128)(2,1)}, bf16[288,192]{1,0:T(8,128)(2,1)}, bf16[288,192]{1,0:T(8,128)(2,1)}, ...) | async-done | bytes 3538960 | tf_op jit(solution)/shard_map/psum | solution.py:340
  (541 shorter events, 182.4 us)
Async XLA Ops:
  7.2 141.5 %all-gather.4.cloned.1.call-start = ((), (), s32[]{:S(2)}) async-start(), calls=%async_computation.7 | async-start | bytes 2654208 | tf_op jit(solution)/shard_map/all_gather | solution.py:100
  8.0 143.7 %all-gather.6.cloned.1.call-start = ((), (), s32[]{:S(2)}) async-start(), calls=%async_computation.8 | async-start | bytes 2654208 | tf_op jit(solution)/shard_map/all_gather | solution.py:101
  8.7 145.8 %all-gather.8.cloned.1.call-start = ((), (), s32[]{:S(2)}) async-start(), calls=%async_computation.9 | async-start | bytes 2654208 | tf_op jit(solution)/shard_map/all_gather | solution.py:102
  9.4 392.2 %reduce-scatter.12.cloned.1.call-start = ((), (), s32[]{:S(2)}) async-start(), calls=%async_computation.12 | async-start | bytes 442368 | tf_op jit(solution)/shard_map/reduce_scatter | solution.py:317
  163.3 14.8 %collective-permute-start = (bf16[2,64,3,64]{3,1,2,0:T(8,128)(2,1)S(1)}, bf16[2,64,3,64]{3,1,2,0:T(8,128)(2,1)S(1)}, u32[]{:S(2)}, u32[]{:S(2)}) collective-permute-start(bf16[2,64,3,64]{3,1,2,0:T(8,128)(2,1)S(1)} %copy.200), channel_id=1, source_target_pairs={{30,0},{0,2},{2,4},{4,6},{6,8},{8,10},{10,12},{12,14},{14,16},{16,... | collective-permute-start | bytes 147464 | tf_op jit(solution)/shard_map/while/body/eval_jaxpr/ppermute | solution.py:17
  164.0 14.1 %collective-permute-start.1 = (bf16[2,64,3,64]{3,1,2,0:T(8,128)(2,1)S(1)}, bf16[2,64,3,64]{3,1,2,0:T(8,128)(2,1)S(1)}, u32[]{:S(2)}, u32[]{:S(2)}) collective-permute-start(bf16[2,64,3,64]{3,1,2,0:T(8,128)(2,1)S(1)} %copy.201), channel_id=1, source_target_pairs={{30,0},{0,2},{2,4},{4,6},{6,8},{8,10},{10,12},{12,14},{14,16},{16,... | collective-permute-start | bytes 147464 | tf_op jit(solution)/shard_map/while/body/eval_jaxpr/ppermute | solution.py:17
  178.2 14.1 %collective-permute-start = (bf16[2,64,3,64]{3,1,2,0:T(8,128)(2,1)S(1)}, bf16[2,64,3,64]{3,1,2,0:T(8,128)(2,1)S(1)}, u32[]{:S(2)}, u32[]{:S(2)}) collective-permute-start(bf16[2,64,3,64]{3,1,2,0:T(8,128)(2,1)S(1)} %copy.200), channel_id=1, source_target_pairs={{30,0},{0,2},{2,4},{4,6},{6,8},{8,10},{10,12},{12,14},{14,16},{16,... | collective-permute-start | bytes 147464 | tf_op jit(solution)/shard_map/while/body/eval_jaxpr/ppermute | solution.py:17
  178.2 14.1 %collective-permute-start.1 = (bf16[2,64,3,64]{3,1,2,0:T(8,128)(2,1)S(1)}, bf16[2,64,3,64]{3,1,2,0:T(8,128)(2,1)S(1)}, u32[]{:S(2)}, u32[]{:S(2)}) collective-permute-start(bf16[2,64,3,64]{3,1,2,0:T(8,128)(2,1)S(1)} %copy.201), channel_id=1, source_target_pairs={{30,0},{0,2},{2,4},{4,6},{6,8},{8,10},{10,12},{12,14},{14,16},{16,... | collective-permute-start | bytes 147464 | tf_op jit(solution)/shard_map/while/body/eval_jaxpr/ppermute | solution.py:17
  192.4 14.1 %collective-permute-start = (bf16[2,64,3,64]{3,1,2,0:T(8,128)(2,1)S(1)}, bf16[2,64,3,64]{3,1,2,0:T(8,128)(2,1)S(1)}, u32[]{:S(2)}, u32[]{:S(2)}) collective-permute-start(bf16[2,64,3,64]{3,1,2,0:T(8,128)(2,1)S(1)} %copy.200), channel_id=1, source_target_pairs={{30,0},{0,2},{2,4},{4,6},{6,8},{8,10},{10,12},{12,14},{14,16},{16,... | collective-permute-start | bytes 147464 | tf_op jit(solution)/shard_map/while/body/eval_jaxpr/ppermute | solution.py:17
  192.4 14.0 %collective-permute-start.1 = (bf16[2,64,3,64]{3,1,2,0:T(8,128)(2,1)S(1)}, bf16[2,64,3,64]{3,1,2,0:T(8,128)(2,1)S(1)}, u32[]{:S(2)}, u32[]{:S(2)}) collective-permute-start(bf16[2,64,3,64]{3,1,2,0:T(8,128)(2,1)S(1)} %copy.201), channel_id=1, source_target_pairs={{30,0},{0,2},{2,4},{4,6},{6,8},{8,10},{10,12},{12,14},{14,16},{16,... | collective-permute-start | bytes 147464 | tf_op jit(solution)/shard_map/while/body/eval_jaxpr/ppermute | solution.py:17
  206.5 14.2 %collective-permute-start = (bf16[2,64,3,64]{3,1,2,0:T(8,128)(2,1)S(1)}, bf16[2,64,3,64]{3,1,2,0:T(8,128)(2,1)S(1)}, u32[]{:S(2)}, u32[]{:S(2)}) collective-permute-start(bf16[2,64,3,64]{3,1,2,0:T(8,128)(2,1)S(1)} %copy.200), channel_id=1, source_target_pairs={{30,0},{0,2},{2,4},{4,6},{6,8},{8,10},{10,12},{12,14},{14,16},{16,... | collective-permute-start | bytes 147464 | tf_op jit(solution)/shard_map/while/body/eval_jaxpr/ppermute | solution.py:17
  206.5 14.2 %collective-permute-start.1 = (bf16[2,64,3,64]{3,1,2,0:T(8,128)(2,1)S(1)}, bf16[2,64,3,64]{3,1,2,0:T(8,128)(2,1)S(1)}, u32[]{:S(2)}, u32[]{:S(2)}) collective-permute-start(bf16[2,64,3,64]{3,1,2,0:T(8,128)(2,1)S(1)} %copy.201), channel_id=1, source_target_pairs={{30,0},{0,2},{2,4},{4,6},{6,8},{8,10},{10,12},{12,14},{14,16},{16,... | collective-permute-start | bytes 147464 | tf_op jit(solution)/shard_map/while/body/eval_jaxpr/ppermute | solution.py:17
  248.1 16.2 %collective-permute-start = (bf16[2,64,3,64]{3,1,2,0:T(8,128)(2,1)S(1)}, bf16[2,64,3,64]{3,1,2,0:T(8,128)(2,1)S(1)}, u32[]{:S(2)}, u32[]{:S(2)}) collective-permute-start(bf16[2,64,3,64]{3,1,2,0:T(8,128)(2,1)S(1)} %copy.200), channel_id=1, source_target_pairs={{30,0},{0,2},{2,4},{4,6},{6,8},{8,10},{10,12},{12,14},{14,16},{16,... | collective-permute-start | bytes 147464 | tf_op jit(solution)/shard_map/while/body/eval_jaxpr/ppermute | solution.py:17
  248.3 16.0 %collective-permute-start.1 = (bf16[2,64,3,64]{3,1,2,0:T(8,128)(2,1)S(1)}, bf16[2,64,3,64]{3,1,2,0:T(8,128)(2,1)S(1)}, u32[]{:S(2)}, u32[]{:S(2)}) collective-permute-start(bf16[2,64,3,64]{3,1,2,0:T(8,128)(2,1)S(1)} %copy.201), channel_id=1, source_target_pairs={{30,0},{0,2},{2,4},{4,6},{6,8},{8,10},{10,12},{12,14},{14,16},{16,... | collective-permute-start | bytes 147464 | tf_op jit(solution)/shard_map/while/body/eval_jaxpr/ppermute | solution.py:17
  264.3 14.5 %collective-permute-start = (bf16[2,64,3,64]{3,1,2,0:T(8,128)(2,1)S(1)}, bf16[2,64,3,64]{3,1,2,0:T(8,128)(2,1)S(1)}, u32[]{:S(2)}, u32[]{:S(2)}) collective-permute-start(bf16[2,64,3,64]{3,1,2,0:T(8,128)(2,1)S(1)} %copy.200), channel_id=1, source_target_pairs={{30,0},{0,2},{2,4},{4,6},{6,8},{8,10},{10,12},{12,14},{14,16},{16,... | collective-permute-start | bytes 147464 | tf_op jit(solution)/shard_map/while/body/eval_jaxpr/ppermute | solution.py:17
  264.4 14.4 %collective-permute-start.1 = (bf16[2,64,3,64]{3,1,2,0:T(8,128)(2,1)S(1)}, bf16[2,64,3,64]{3,1,2,0:T(8,128)(2,1)S(1)}, u32[]{:S(2)}, u32[]{:S(2)}) collective-permute-start(bf16[2,64,3,64]{3,1,2,0:T(8,128)(2,1)S(1)} %copy.201), channel_id=1, source_target_pairs={{30,0},{0,2},{2,4},{4,6},{6,8},{8,10},{10,12},{12,14},{14,16},{16,... | collective-permute-start | bytes 147464 | tf_op jit(solution)/shard_map/while/body/eval_jaxpr/ppermute | solution.py:17
  278.9 15.0 %collective-permute-start = (bf16[2,64,3,64]{3,1,2,0:T(8,128)(2,1)S(1)}, bf16[2,64,3,64]{3,1,2,0:T(8,128)(2,1)S(1)}, u32[]{:S(2)}, u32[]{:S(2)}) collective-permute-start(bf16[2,64,3,64]{3,1,2,0:T(8,128)(2,1)S(1)} %copy.200), channel_id=1, source_target_pairs={{30,0},{0,2},{2,4},{4,6},{6,8},{8,10},{10,12},{12,14},{14,16},{16,... | collective-permute-start | bytes 147464 | tf_op jit(solution)/shard_map/while/body/eval_jaxpr/ppermute | solution.py:17
  279.0 15.0 %collective-permute-start.1 = (bf16[2,64,3,64]{3,1,2,0:T(8,128)(2,1)S(1)}, bf16[2,64,3,64]{3,1,2,0:T(8,128)(2,1)S(1)}, u32[]{:S(2)}, u32[]{:S(2)}) collective-permute-start(bf16[2,64,3,64]{3,1,2,0:T(8,128)(2,1)S(1)} %copy.201), channel_id=1, source_target_pairs={{30,0},{0,2},{2,4},{4,6},{6,8},{8,10},{10,12},{12,14},{14,16},{16,... | collective-permute-start | bytes 147464 | tf_op jit(solution)/shard_map/while/body/eval_jaxpr/ppermute | solution.py:17
  294.0 15.4 %collective-permute-start = (bf16[2,64,3,64]{3,1,2,0:T(8,128)(2,1)S(1)}, bf16[2,64,3,64]{3,1,2,0:T(8,128)(2,1)S(1)}, u32[]{:S(2)}, u32[]{:S(2)}) collective-permute-start(bf16[2,64,3,64]{3,1,2,0:T(8,128)(2,1)S(1)} %copy.200), channel_id=1, source_target_pairs={{30,0},{0,2},{2,4},{4,6},{6,8},{8,10},{10,12},{12,14},{14,16},{16,... | collective-permute-start | bytes 147464 | tf_op jit(solution)/shard_map/while/body/eval_jaxpr/ppermute | solution.py:17
  294.1 15.4 %collective-permute-start.1 = (bf16[2,64,3,64]{3,1,2,0:T(8,128)(2,1)S(1)}, bf16[2,64,3,64]{3,1,2,0:T(8,128)(2,1)S(1)}, u32[]{:S(2)}, u32[]{:S(2)}) collective-permute-start(bf16[2,64,3,64]{3,1,2,0:T(8,128)(2,1)S(1)} %copy.201), channel_id=1, source_target_pairs={{30,0},{0,2},{2,4},{4,6},{6,8},{8,10},{10,12},{12,14},{14,16},{16,... | collective-permute-start | bytes 147464 | tf_op jit(solution)/shard_map/while/body/eval_jaxpr/ppermute | solution.py:17
  309.5 14.8 %collective-permute-start = (bf16[2,64,3,64]{3,1,2,0:T(8,128)(2,1)S(1)}, bf16[2,64,3,64]{3,1,2,0:T(8,128)(2,1)S(1)}, u32[]{:S(2)}, u32[]{:S(2)}) collective-permute-start(bf16[2,64,3,64]{3,1,2,0:T(8,128)(2,1)S(1)} %copy.200), channel_id=1, source_target_pairs={{30,0},{0,2},{2,4},{4,6},{6,8},{8,10},{10,12},{12,14},{14,16},{16,... | collective-permute-start | bytes 147464 | tf_op jit(solution)/shard_map/while/body/eval_jaxpr/ppermute | solution.py:17
  309.5 14.7 %collective-permute-start.1 = (bf16[2,64,3,64]{3,1,2,0:T(8,128)(2,1)S(1)}, bf16[2,64,3,64]{3,1,2,0:T(8,128)(2,1)S(1)}, u32[]{:S(2)}, u32[]{:S(2)}) collective-permute-start(bf16[2,64,3,64]{3,1,2,0:T(8,128)(2,1)S(1)} %copy.201), channel_id=1, source_target_pairs={{30,0},{0,2},{2,4},{4,6},{6,8},{8,10},{10,12},{12,14},{14,16},{16,... | collective-permute-start | bytes 147464 | tf_op jit(solution)/shard_map/while/body/eval_jaxpr/ppermute | solution.py:17
  324.3 14.1 %collective-permute-start = (bf16[2,64,3,64]{3,1,2,0:T(8,128)(2,1)S(1)}, bf16[2,64,3,64]{3,1,2,0:T(8,128)(2,1)S(1)}, u32[]{:S(2)}, u32[]{:S(2)}) collective-permute-start(bf16[2,64,3,64]{3,1,2,0:T(8,128)(2,1)S(1)} %copy.200), channel_id=1, source_target_pairs={{30,0},{0,2},{2,4},{4,6},{6,8},{8,10},{10,12},{12,14},{14,16},{16,... | collective-permute-start | bytes 147464 | tf_op jit(solution)/shard_map/while/body/eval_jaxpr/ppermute | solution.py:17
  324.4 14.0 %collective-permute-start.1 = (bf16[2,64,3,64]{3,1,2,0:T(8,128)(2,1)S(1)}, bf16[2,64,3,64]{3,1,2,0:T(8,128)(2,1)S(1)}, u32[]{:S(2)}, u32[]{:S(2)}) collective-permute-start(bf16[2,64,3,64]{3,1,2,0:T(8,128)(2,1)S(1)} %copy.201), channel_id=1, source_target_pairs={{30,0},{0,2},{2,4},{4,6},{6,8},{8,10},{10,12},{12,14},{14,16},{16,... | collective-permute-start | bytes 147464 | tf_op jit(solution)/shard_map/while/body/eval_jaxpr/ppermute | solution.py:17
  338.4 13.9 %collective-permute-start = (bf16[2,64,3,64]{3,1,2,0:T(8,128)(2,1)S(1)}, bf16[2,64,3,64]{3,1,2,0:T(8,128)(2,1)S(1)}, u32[]{:S(2)}, u32[]{:S(2)}) collective-permute-start(bf16[2,64,3,64]{3,1,2,0:T(8,128)(2,1)S(1)} %copy.200), channel_id=1, source_target_pairs={{30,0},{0,2},{2,4},{4,6},{6,8},{8,10},{10,12},{12,14},{14,16},{16,... | collective-permute-start | bytes 147464 | tf_op jit(solution)/shard_map/while/body/eval_jaxpr/ppermute | solution.py:17
  390.3 15.0 %reduce-scatter.10.cloned.1.call-start = ((), (), s32[]{:S(2)}) async-start(), calls=%async_computation.11 | async-start | bytes 442368 | tf_op jit(solution)/shard_map/reduce_scatter | solution.py:314
  391.7 25.1 %reduce-scatter.14.cloned.1.call-start = ((), (), s32[]{:S(2)}) async-start(), calls=%async_computation.13 | async-start | bytes 1105920 | tf_op jit(solution)/shard_map/reduce_scatter | solution.py:320
  393.0 36.0 %reduce-scatter.8.cloned.1.call-start = ((), (), s32[]{:S(2)}) async-start(), calls=%async_computation.10 | async-start | bytes 1105920 | tf_op jit(solution)/shard_map/reduce_scatter | solution.py:311
  395.5 46.8 %reduce-scatter.18.cloned.1.call-start = ((), (), s32[]{:S(2)}) async-start(), calls=%async_computation.15 | async-start | bytes 2654208 | tf_op jit(solution)/shard_map/reduce_scatter | solution.py:329
  397.5 58.3 %reduce-scatter.16.cloned.1.call-start = ((), (), s32[]{:S(2)}) async-start(), calls=%async_computation.14 | async-start | bytes 2654208 | tf_op jit(solution)/shard_map/reduce_scatter | solution.py:326
  399.4 69.6 %reduce-scatter.20.cloned.1.call-start = ((), (), s32[]{:S(2)}) async-start(), calls=%async_computation.16 | async-start | bytes 2654208 | tf_op jit(solution)/shard_map/reduce_scatter | solution.py:332
  401.3 238.7 %all-reduce.10.cloned.1.call-start = ((), (), s32[]{:S(2)}) async-start(), calls=%async_computation.17 | async-start | bytes 7372800 | tf_op jit(solution)/shard_map/psum | solution.py:340
  (92 other events, 991.8 us)
Sparse Core Ops, SparseCore 0:
  9.6 12.7 all-gather.3
  24.0 11.2 all-gather.5
  36.8 11.2 all-gather.7
  390.5 3.8 reduce-scatter.11
  396.4 8.8 reduce-scatter.9
  407.4 9.3 reduce-scatter.13
  419.6 9.3 reduce-scatter.7
  431.9 10.4 reduce-scatter.17
  445.3 10.4 reduce-scatter.15
  458.5 10.4 reduce-scatter.19
  476.6 163.4 all-reduce.9
where the time goes:
time: 657 us; the launch traced here: 655 us
  waiting for transfers between devices  310 us (47%)
  blocking collectives  162 us (25%)
  matrix products  68.4 us (10%)
  other arithmetic  44.1 us (7%)
  starting transfers between devices  41.7 us (6%)
  between operations  16.2 us (2%)
  local copies, waits for them, and re-layouts  10.6 us (2%)
    ppermute x62, waiting for transfers between devices, shifted(): return lax.ppermute(block, axis, route)  123 us
    psum x1, waiting for transfers between devices, local(): lax.psum(owned_grads[0].astype(jnp.bfloat16), 'ctx').astype(jnp.float32)  118 us
    all_gather x1, blocking collectives, local(): key_part = lax.all_gather(key_rows, 'ctx', axis=1, tiled=True)  54.9 us
    all_gather x1, blocking collectives, local(): value_part = lax.all_gather(value_rows, 'ctx', axis=1, tiled=True)  49.6 us
    psum x1, blocking collectives, local(): lax.psum(owned_grads[4].astype(jnp.bfloat16), 'ctx').astype(jnp.float32)  43.7 us
    ppermute x62, starting transfers between devices, shifted(): return lax.ppermute(block, axis, route)  41 us
    dot_general x16, matrix products, block_grads(): jnp.einsum('sqkgd,snkd->skgqn', queries, key_part, preferred_element_type...  17 us
    reduce_scatter x1, waiting for transfers between devices, local(): lax.psum_scatter(grad_wgate.astype(jnp.bfloat16), 'fsdp', scatter_dimensi...  13.4 us
  transfers between devices with their start and end apart: 73, of which 38 were waited for; matrix products, arithmetic and copies ran while one was open for 16% of the time, Pallas kernels for 0%

commit v1 on v0

--- a/solution.py
+++ b/solution.py
@@ -147,7 +147,12 @@
     stat_shape = (seq_count, KV_HEADS, group_size, tok_count)
     running_max = jnp.full(stat_shape, masked_value, jnp.float32)
     key_part = lax.all_gather(key_rows, "ctx", axis=1, tiled=True)
-    value_part = lax.all_gather(value_rows, "ctx", axis=1, tiled=True)
+    ring = [value_rows]
+    for hop in range(15):
+        ring.append(lax.ppermute(ring[-1], "ctx", [(dev, (dev + 1) % 16) for dev in range(16)]))
+    value_part = jnp.roll(
+        jnp.concatenate(ring[::-1], axis=1), (lax.axis_index("ctx") + 1) * ring[0].shape[1], axis=1
+    )
     key_pos = slot_positions(block_of_slot, jnp.int32(0), key_part.shape[1], half_len)
     visible = query_pos[:, None] >= key_pos[None, :]
     scores = (

time: 657 us -> 717 us (1.091)
  waiting for transfers between devices: 310 us -> 401 us
  blocking collectives: 162 us -> 108 us
  starting transfers between devices: 41.7 us -> 57.8 us
  local copies, waits for them, and re-layouts: 10.6 us -> 18 us
    ppermute x0 -> x15, waiting for transfers between devices: none -> 105 us  [local(): lax.ppermute(ring[-1], 'ctx', [(dev, (dev + 1) % 16) for dev in range(16)])]
    all_gather x1 -> x0, blocking collectives: 49.6 us -> none  [local(): value_part = lax.all_gather(value_rows, 'ctx', axis=1, tiled=True)]
    ppermute x62, waiting for transfers between devices: 123 us -> 109 us  [shifted(): return lax.ppermute(block, axis, route)]
    ppermute x62, starting transfers between devices: 41 us -> 54.1 us  [shifted(): return lax.ppermute(block, axis, route)]
  transfers between devices with their start and end apart: 73 -> 88, of which waited for: 38 -> 52; matrix products, arithmetic and copies ran while one was open for 16% -> 15% of each run, Pallas kernels for 0% -> 0%
where the time goes in v1:
time: 717 us; the launch traced here: 715 us
  waiting for transfers between devices  401 us (56%)
  blocking collectives  108 us (15%)
  matrix products  68.9 us (10%)
  starting transfers between devices  57.8 us (8%)
  other arithmetic  42.2 us (6%)
  local copies, waits for them, and re-layouts  18 us (3%)
  between operations  16.4 us (2%)
    psum x1, waiting for transfers between devices, local(): lax.psum(owned_grads[0].astype(jnp.bfloat16), 'ctx').astype(jnp.float32)  118 us
    ppermute x62, waiting for transfers between devices, shifted(): return lax.ppermute(block, axis, route)  109 us
    ppermute x15, waiting for transfers between devices, local(): lax.ppermute(ring[-1], 'ctx', [(dev, (dev + 1) % 16) for dev in range(16)])  105 us
    ppermute x62, starting transfers between devices, shifted(): return lax.ppermute(block, axis, route)  54.1 us
    all_gather x1, blocking collectives, local(): key_part = lax.all_gather(key_rows, 'ctx', axis=1, tiled=True)  50.5 us
    psum x1, blocking collectives, local(): lax.psum(owned_grads[4].astype(jnp.bfloat16), 'ctx').astype(jnp.float32)  43.7 us
    dot_general x16, matrix products, block_grads(): jnp.einsum('sqkgd,snkd->skgqn', queries, key_part, preferred_element_type...  17 us
  transfers between devices with their start and end apart: 88, of which 52 were waited for; matrix products, arithmetic and copies ran while one was open for 15% of the time, Pallas kernels for 0%

profile of v1, /device:TPU:0, one launch (start us, length us, event | category | flops | bytes accessed | tf_op | source)
XLA Modules:
  0.0 714.6 jit_solution(2410887008916072973)
XLA Ops:
  25.6 50.5 %all_gather.32 = bf16[2,1024,3,64]{3,0,2,1:T(2,128)(2,1)S(1)} all-gather(bf16[2,64,3,64]{3,0,2,1:T(2,128)(2,1)S(1)} %copy.120), channel_id=1, replica_groups=mesh['ctx'=16,'fsdp'=2] {'ctx'}, dimensions={1}, use_global_device_ids=true | all-gather | bytes 835584 | tf_op jit(solution)/shard_map/all_gather | solution.py:149
  79.3 8.2 %collective-permute-done.5 = bf16[2,64,3,64]{1,3,2,0:T(8,128)(2,1)S(1)} collective-permute-done((bf16[2,64,3,64]{1,3,2,0:T(8,128)(2,1)}, bf16[2,64,3,64]{1,3,2,0:T(8,128)(2,1)S(1)}, u32[]{:S(2)}, u32[]{:S(2)}) %collective-permute-start.5) | collective-permute-done | bytes 49184 | tf_op jit(solution)/shard_map/ppermute | solution.py:152
  87.6 8.1 %collective-permute-done.6 = bf16[2,64,3,64]{1,3,2,0:T(8,128)(2,1)S(1)} collective-permute-done((bf16[2,64,3,64]{1,3,2,0:T(8,128)(2,1)S(1)}, bf16[2,64,3,64]{1,3,2,0:T(8,128)(2,1)S(1)}, u32[]{:S(2)}, u32[]{:S(2)}) %collective-permute-start.6) | collective-permute-done | bytes 49184 | tf_op jit(solution)/shard_map/ppermute | solution.py:152
  95.7 8.2 %collective-permute-done.7 = bf16[2,64,3,64]{1,3,2,0:T(8,128)(2,1)S(1)} collective-permute-done((bf16[2,64,3,64]{1,3,2,0:T(8,128)(2,1)S(1)}, bf16[2,64,3,64]{1,3,2,0:T(8,128)(2,1)S(1)}, u32[]{:S(2)}, u32[]{:S(2)}) %collective-permute-start.7) | collective-permute-done | bytes 49184 | tf_op jit(solution)/shard_map/ppermute | solution.py:152
  104.7 7.4 %collective-permute-done.8 = bf16[2,64,3,64]{1,3,2,0:T(8,128)(2,1)S(1)} collective-permute-done((bf16[2,64,3,64]{1,3,2,0:T(8,128)(2,1)S(1)}, bf16[2,64,3,64]{1,3,2,0:T(8,128)(2,1)S(1)}, u32[]{:S(2)}, u32[]{:S(2)}) %collective-permute-start.8) | collective-permute-done | bytes 49184 | tf_op jit(solution)/shard_map/ppermute | solution.py:152
  112.2 8.2 %collective-permute-done.9 = bf16[2,64,3,64]{1,3,2,0:T(8,128)(2,1)S(1)} collective-permute-done((bf16[2,64,3,64]{1,3,2,0:T(8,128)(2,1)S(1)}, bf16[2,64,3,64]{1,3,2,0:T(8,128)(2,1)S(1)}, u32[]{:S(2)}, u32[]{:S(2)}) %collective-permute-start.9) | collective-permute-done | bytes 49184 | tf_op jit(solution)/shard_map/ppermute | solution.py:152
  121.6 7.2 %collective-permute-done.10 = bf16[2,64,3,64]{1,3,2,0:T(8,128)(2,1)S(1)} collective-permute-done((bf16[2,64,3,64]{1,3,2,0:T(8,128)(2,1)S(1)}, bf16[2,64,3,64]{1,3,2,0:T(8,128)(2,1)S(1)}, u32[]{:S(2)}, u32[]{:S(2)}) %collective-permute-start.10) | collective-permute-done | bytes 49184 | tf_op jit(solution)/shard_map/ppermute | solution.py:152
  129.0 8.7 %collective-permute-done.11 = bf16[2,64,3,64]{1,3,2,0:T(8,128)(2,1)S(1)} collective-permute-done((bf16[2,64,3,64]{1,3,2,0:T(8,128)(2,1)S(1)}, bf16[2,64,3,64]{1,3,2,0:T(8,128)(2,1)S(1)}, u32[]{:S(2)}, u32[]{:S(2)}) %collective-permute-start.11) | collective-permute-done | bytes 49184 | tf_op jit(solution)/shard_map/ppermute | solution.py:152
  138.8 7.2 %collective-permute-done.12 = bf16[2,64,3,64]{1,3,2,0:T(8,128)(2,1)S(1)} collective-permute-done((bf16[2,64,3,64]{1,3,2,0:T(8,128)(2,1)S(1)}, bf16[2,64,3,64]{1,3,2,0:T(8,128)(2,1)S(1)}, u32[]{:S(2)}, u32[]{:S(2)}) %collective-permute-start.12) | collective-permute-done | bytes 49184 | tf_op jit(solution)/shard_map/ppermute | solution.py:152
  146.0 8.2 %collective-permute-done.13 = bf16[2,64,3,64]{1,3,2,0:T(8,128)(2,1)S(1)} collective-permute-done((bf16[2,64,3,64]{1,3,2,0:T(8,128)(2,1)S(1)}, bf16[2,64,3,64]{1,3,2,0:T(8,128)(2,1)S(1)}, u32[]{:S(2)}, u32[]{:S(2)}) %collective-permute-start.13) | collective-permute-done | bytes 49184 | tf_op jit(solution)/shard_map/ppermute | solution.py:152
  155.8 6.6 collective-permute-done.14
  163.0 7.6 %collective-permute-done.15 = bf16[2,64,3,64]{1,3,2,0:T(8,128)(2,1)S(1)} collective-permute-done((bf16[2,64,3,64]{1,3,2,0:T(8,128)(2,1)S(1)}, bf16[2,64,3,64]{1,3,2,0:T(8,128)(2,1)S(1)}, u32[]{:S(2)}, u32[]{:S(2)}) %collective-permute-start.15) | collective-permute-done | bytes 49184 | tf_op jit(solution)/shard_map/ppermute | solution.py:152
  170.6 8.2 %collective-permute-done.16 = bf16[2,64,3,64]{1,3,2,0:T(8,128)(2,1)S(1)} collective-permute-done((bf16[2,64,3,64]{1,3,2,0:T(8,128)(2,1)S(1)}, bf16[2,64,3,64]{1,3,2,0:T(8,128)(2,1)S(1)}, u32[]{:S(2)}, u32[]{:S(2)}) %collective-permute-start.16) | collective-permute-done | bytes 49184 | tf_op jit(solution)/shard_map/ppermute | solution.py:152
  180.2 7.0 collective-permute-done.17
  195.7 6.4 concatenate.29
  222.8 215.6 %while.25 = (s32[]{:T(128)}, bf16[2,64,3,64]{3,1,2,0:T(8,128)(2,1)S(1)}, bf16[2,64,3,64]{3,1,2,0:T(8,128)(2,1)S(1)}, f32[2,3,3,64,64]{4,3,2,1,0:T(8,128)S(1)}, f...) while((s32[]{:T(128)}, ...), condition=%wide.region_10.11_spmd.clone, body=%wide.region_8.10_spmd.clone.sunk | while | flops 48082768 | bytes 4246918 | solution.py:262
  227.0 7.5 %collective-permute-done.2 = bf16[2,64,3,64]{3,1,2,0:T(8,128)(2,1)S(1)} collective-permute-done((bf16[2,64,3,64]{3,1,2,0:T(8,128)(2,1)S(1)}, bf16[2,64,3,64]{3,1,2,0:T(8,128)(2,1)S(1)}, u32[]{:S(2)}, u32[]{:S(2)}) %collective-permute-start.2) | collective-permute-done | bytes 49184 | tf_op jit(solution)/shard_map/while/body/eval_jaxpr/ppermute | solution.py:17
  239.8 7.5 %collective-permute-done.2 = bf16[2,64,3,64]{3,1,2,0:T(8,128)(2,1)S(1)} collective-permute-done((bf16[2,64,3,64]{3,1,2,0:T(8,128)(2,1)S(1)}, bf16[2,64,3,64]{3,1,2,0:T(8,128)(2,1)S(1)}, u32[]{:S(2)}, u32[]{:S(2)}) %collective-permute-start.2) | collective-permute-done | bytes 49184 | tf_op jit(solution)/shard_map/while/body/eval_jaxpr/ppermute | solution.py:17
  252.6 7.5 %collective-permute-done.2 = bf16[2,64,3,64]{3,1,2,0:T(8,128)(2,1)S(1)} collective-permute-done((bf16[2,64,3,64]{3,1,2,0:T(8,128)(2,1)S(1)}, bf16[2,64,3,64]{3,1,2,0:T(8,128)(2,1)S(1)}, u32[]{:S(2)}, u32[]{:S(2)}) %collective-permute-start.2) | collective-permute-done | bytes 49184 | tf_op jit(solution)/shard_map/while/body/eval_jaxpr/ppermute | solution.py:17
  330.6 5.8 collective-permute-done.2
  342.9 6.6 collective-permute-done.2
  355.5 7.7 %collective-permute-done.2 = bf16[2,64,3,64]{3,1,2,0:T(8,128)(2,1)S(1)} collective-permute-done((bf16[2,64,3,64]{3,1,2,0:T(8,128)(2,1)S(1)}, bf16[2,64,3,64]{3,1,2,0:T(8,128)(2,1)S(1)}, u32[]{:S(2)}, u32[]{:S(2)}) %collective-permute-start.2) | collective-permute-done | bytes 49184 | tf_op jit(solution)/shard_map/while/body/eval_jaxpr/ppermute | solution.py:17
  416.5 7.8 %collective-permute-done.2 = bf16[2,64,3,64]{3,1,2,0:T(8,128)(2,1)S(1)} collective-permute-done((bf16[2,64,3,64]{3,1,2,0:T(8,128)(2,1)S(1)}, bf16[2,64,3,64]{3,1,2,0:T(8,128)(2,1)S(1)}, u32[]{:S(2)}, u32[]{:S(2)}) %collective-permute-start.2) | collective-permute-done | bytes 49184 | tf_op jit(solution)/shard_map/while/body/eval_jaxpr/ppermute | solution.py:17
  429.8 7.4 %collective-permute-done.2 = bf16[2,64,3,64]{3,1,2,0:T(8,128)(2,1)S(1)} collective-permute-done((bf16[2,64,3,64]{3,1,2,0:T(8,128)(2,1)S(1)}, bf16[2,64,3,64]{3,1,2,0:T(8,128)(2,1)S(1)}, u32[]{:S(2)}, u32[]{:S(2)}) %collective-permute-start.2) | collective-permute-done | bytes 49184 | tf_op jit(solution)/shard_map/while/body/eval_jaxpr/ppermute | solution.py:17
  440.6 7.4 %collective-permute-done.20 = bf16[2,64,3,64]{1,3,2,0:T(8,128)(2,1)S(1)} collective-permute-done((bf16[2,64,3,64]{1,3,2,0:T(8,128)(2,1)S(1)}, bf16[2,64,3,64]{1,3,2,0:T(8,128)(2,1)S(1)}, u32[]{:S(2)}, u32[]{:S(2)}) %collective-permute-start.20) | collective-permute-done | bytes 49184 | tf_op jit(solution)/shard_map/ppermute | solution.py:17
  464.6 11.5 %reduce-scatter.14.cloned.1.call-done = bf16[288,576]{1,0:T(8,128)(2,1)} async-done(((bf16[576,576]{1,0:T(8,128)(2,1)}), bf16[288,576]{1,0:T(8,128)(2,1)}) %reduce-scatter.14.cloned.1.call-update) | async-done | bytes 331792 | tf_op jit(solution)/shard_map/reduce_scatter | solution.py:325
  476.1 12.2 %reduce-scatter.8.cloned.1.call-done = bf16[288,576]{1,0:T(8,128)(2,1)} async-done(((bf16[576,576]{1,0:T(8,128)(2,1)}), bf16[288,576]{1,0:T(8,128)(2,1)}) %reduce-scatter.8.cloned.1.call-update) | async-done | bytes 331792 | tf_op jit(solution)/shard_map/reduce_scatter | solution.py:316
  488.3 13.3 %reduce-scatter.18.cloned.1.call-done = bf16[288,1536]{1,0:T(8,128)(2,1)} async-done(((bf16[576,1536]{1,0:T(8,128)(2,1)}), bf16[288,1536]{1,0:T(8,128)(2,1)}) %reduce-scatter.18.cloned.1.call-update) | async-done | bytes 884752 | tf_op jit(solution)/shard_map/reduce_scatter | solution.py:334
  501.7 13.4 %reduce-scatter.16.cloned.1.call-done = bf16[288,1536]{1,0:T(8,128)(2,1)} async-done(((bf16[576,1536]{1,0:T(8,128)(2,1)}), bf16[288,1536]{1,0:T(8,128)(2,1)}) %reduce-scatter.16.cloned.1.call-update) | async-done | bytes 884752 | tf_op jit(solution)/shard_map/reduce_scatter | solution.py:331
  515.1 13.2 %reduce-scatter.20.cloned.1.call-done = bf16[768,576]{0,1:T(8,128)(2,1)} async-done(((bf16[1536,576]{0,1:T(8,128)(2,1)}), bf16[768,576]{0,1:T(8,128)(2,1)}) %reduce-scatter.20.cloned.1.call-update) | async-done | bytes 884752 | tf_op jit(solution)/shard_map/reduce_scatter | solution.py:337
  535.6 43.7 %all-reduce.4 = (bf16[288]{0:T(512)(128)(2,1)S(1)}, bf16[288]{0:T(512)(128)(2,1)S(1)}) all-reduce(bf16[288]{0:T(512)(128)(2,1)S(1)} %dynamic-slice.3, bf16[288]{0:T(512)(128)(2,1)S(1)} %dynamic-slice.5), channel_id=1, replica_groups=mesh['ctx'=16,'fsdp'=2] {'ctx'}, use_global_device_ids=true, to_apply=%region_23.24 | all-reduce | flops 576 | bytes 2304 | tf_op jit(solution)/shard_map/psum | solution.py:349
  581.5 117.9 %all-reduce.10.cloned.1.call-done = (bf16[288,576]{1,0:T(8,128)(2,1)}, bf16[288,192]{1,0:T(8,128)(2,1)}, bf16[288,192]{1,0:T(8,128)(2,1)}, bf16[288,576]{1,0:T(8...) async-done(((bf16[288,576]{1,0:T(8,128)(2,1)}, bf16[288,192]{1,0:T(8,128)(2,1)}, bf16[288,192]{1,0:T(8,128)(2,1)}, ...) | async-done | bytes 3538960 | tf_op jit(solution)/shard_map/psum | solution.py:345
  (617 shorter events, 248.2 us)
Async XLA Ops:
  7.2 201.0 %all-gather.4.cloned.1.call-start = ((), (), s32[]{:S(2)}) async-start(), calls=%async_computation.7 | async-start | bytes 2654208 | tf_op jit(solution)/shard_map/all_gather | solution.py:100
  8.0 203.2 %all-gather.6.cloned.1.call-start = ((), (), s32[]{:S(2)}) async-start(), calls=%async_computation.8 | async-start | bytes 2654208 | tf_op jit(solution)/shard_map/all_gather | solution.py:101
  8.7 205.3 %all-gather.8.cloned.1.call-start = ((), (), s32[]{:S(2)}) async-start(), calls=%async_computation.9 | async-start | bytes 2654208 | tf_op jit(solution)/shard_map/all_gather | solution.py:102
  17.4 61.4 %collective-permute-start.4 = (bf16[2,64,3,64]{1,3,2,0:T(8,128)(2,1)}, bf16[2,64,3,64]{1,3,2,0:T(8,128)(2,1)}, u32[]{:S(2)}, u32[]{:S(2)}) collective-permute-start(bf16[2,64,3,64]{1,3,2,0:T(8,128)(2,1)} %copy.126), channel_id=1, source_target_pairs={{0,2},{2,4},{4,6},{6,8},{8,10},{10,12},{12,14},{14,16},{16,18},{18... | collective-permute-start | bytes 147464 | tf_op jit(solution)/shard_map/ppermute | solution.py:152
  20.2 440.4 %reduce-scatter.12.cloned.1.call-start = ((), (), s32[]{:S(2)}) async-start(), calls=%async_computation.12 | async-start | bytes 442368 | tf_op jit(solution)/shard_map/reduce_scatter | solution.py:322
  261.2 13.4 %collective-permute-start = (bf16[2,64,3,64]{3,1,2,0:T(8,128)(2,1)S(1)}, bf16[2,64,3,64]{3,1,2,0:T(8,128)(2,1)S(1)}, u32[]{:S(2)}, u32[]{:S(2)}) collective-permute-start(bf16[2,64,3,64]{3,1,2,0:T(8,128)(2,1)S(1)} %copy.200), channel_id=1, source_target_pairs={{30,0},{0,2},{2,4},{4,6},{6,8},{8,10},{10,12},{12,14},{14,16},{16,... | collective-permute-start | bytes 147464 | tf_op jit(solution)/shard_map/while/body/eval_jaxpr/ppermute | solution.py:17
  261.3 13.3 %collective-permute-start.1 = (bf16[2,64,3,64]{3,1,2,0:T(8,128)(2,1)S(1)}, bf16[2,64,3,64]{3,1,2,0:T(8,128)(2,1)S(1)}, u32[]{:S(2)}, u32[]{:S(2)}) collective-permute-start(bf16[2,64,3,64]{3,1,2,0:T(8,128)(2,1)S(1)} %copy.201), channel_id=1, source_target_pairs={{30,0},{0,2},{2,4},{4,6},{6,8},{8,10},{10,12},{12,14},{14,16},{16,... | collective-permute-start | bytes 147464 | tf_op jit(solution)/shard_map/while/body/eval_jaxpr/ppermute | solution.py:17
  274.6 16.8 %collective-permute-start = (bf16[2,64,3,64]{3,1,2,0:T(8,128)(2,1)S(1)}, bf16[2,64,3,64]{3,1,2,0:T(8,128)(2,1)S(1)}, u32[]{:S(2)}, u32[]{:S(2)}) collective-permute-start(bf16[2,64,3,64]{3,1,2,0:T(8,128)(2,1)S(1)} %copy.200), channel_id=1, source_target_pairs={{30,0},{0,2},{2,4},{4,6},{6,8},{8,10},{10,12},{12,14},{14,16},{16,... | collective-permute-start | bytes 147464 | tf_op jit(solution)/shard_map/while/body/eval_jaxpr/ppermute | solution.py:17
  274.7 16.7 %collective-permute-start.1 = (bf16[2,64,3,64]{3,1,2,0:T(8,128)(2,1)S(1)}, bf16[2,64,3,64]{3,1,2,0:T(8,128)(2,1)S(1)}, u32[]{:S(2)}, u32[]{:S(2)}) collective-permute-start(bf16[2,64,3,64]{3,1,2,0:T(8,128)(2,1)S(1)} %copy.201), channel_id=1, source_target_pairs={{30,0},{0,2},{2,4},{4,6},{6,8},{8,10},{10,12},{12,14},{14,16},{16,... | collective-permute-start | bytes 147464 | tf_op jit(solution)/shard_map/while/body/eval_jaxpr/ppermute | solution.py:17
  291.5 18.3 %collective-permute-start = (bf16[2,64,3,64]{3,1,2,0:T(8,128)(2,1)S(1)}, bf16[2,64,3,64]{3,1,2,0:T(8,128)(2,1)S(1)}, u32[]{:S(2)}, u32[]{:S(2)}) collective-permute-start(bf16[2,64,3,64]{3,1,2,0:T(8,128)(2,1)S(1)} %copy.200), channel_id=1, source_target_pairs={{30,0},{0,2},{2,4},{4,6},{6,8},{8,10},{10,12},{12,14},{14,16},{16,... | collective-permute-start | bytes 147464 | tf_op jit(solution)/shard_map/while/body/eval_jaxpr/ppermute | solution.py:17
  293.4 16.4 %collective-permute-start.1 = (bf16[2,64,3,64]{3,1,2,0:T(8,128)(2,1)S(1)}, bf16[2,64,3,64]{3,1,2,0:T(8,128)(2,1)S(1)}, u32[]{:S(2)}, u32[]{:S(2)}) collective-permute-start(bf16[2,64,3,64]{3,1,2,0:T(8,128)(2,1)S(1)} %copy.201), channel_id=1, source_target_pairs={{30,0},{0,2},{2,4},{4,6},{6,8},{8,10},{10,12},{12,14},{14,16},{16,... | collective-permute-start | bytes 147464 | tf_op jit(solution)/shard_map/while/body/eval_jaxpr/ppermute | solution.py:17
  309.9 14.3 %collective-permute-start = (bf16[2,64,3,64]{3,1,2,0:T(8,128)(2,1)S(1)}, bf16[2,64,3,64]{3,1,2,0:T(8,128)(2,1)S(1)}, u32[]{:S(2)}, u32[]{:S(2)}) collective-permute-start(bf16[2,64,3,64]{3,1,2,0:T(8,128)(2,1)S(1)} %copy.200), channel_id=1, source_target_pairs={{30,0},{0,2},{2,4},{4,6},{6,8},{8,10},{10,12},{12,14},{14,16},{16,... | collective-permute-start | bytes 147464 | tf_op jit(solution)/shard_map/while/body/eval_jaxpr/ppermute | solution.py:17
  309.9 14.3 %collective-permute-start.1 = (bf16[2,64,3,64]{3,1,2,0:T(8,128)(2,1)S(1)}, bf16[2,64,3,64]{3,1,2,0:T(8,128)(2,1)S(1)}, u32[]{:S(2)}, u32[]{:S(2)}) collective-permute-start(bf16[2,64,3,64]{3,1,2,0:T(8,128)(2,1)S(1)} %copy.201), channel_id=1, source_target_pairs={{30,0},{0,2},{2,4},{4,6},{6,8},{8,10},{10,12},{12,14},{14,16},{16,... | collective-permute-start | bytes 147464 | tf_op jit(solution)/shard_map/while/body/eval_jaxpr/ppermute | solution.py:17
  324.3 13.1 %collective-permute-start = (bf16[2,64,3,64]{3,1,2,0:T(8,128)(2,1)S(1)}, bf16[2,64,3,64]{3,1,2,0:T(8,128)(2,1)S(1)}, u32[]{:S(2)}, u32[]{:S(2)}) collective-permute-start(bf16[2,64,3,64]{3,1,2,0:T(8,128)(2,1)S(1)} %copy.200), channel_id=1, source_target_pairs={{30,0},{0,2},{2,4},{4,6},{6,8},{8,10},{10,12},{12,14},{14,16},{16,... | collective-permute-start | bytes 147464 | tf_op jit(solution)/shard_map/while/body/eval_jaxpr/ppermute | solution.py:17
  337.5 13.1 %collective-permute-start = (bf16[2,64,3,64]{3,1,2,0:T(8,128)(2,1)S(1)}, bf16[2,64,3,64]{3,1,2,0:T(8,128)(2,1)S(1)}, u32[]{:S(2)}, u32[]{:S(2)}) collective-permute-start(bf16[2,64,3,64]{3,1,2,0:T(8,128)(2,1)S(1)} %copy.200), channel_id=1, source_target_pairs={{30,0},{0,2},{2,4},{4,6},{6,8},{8,10},{10,12},{12,14},{14,16},{16,... | collective-permute-start | bytes 147464 | tf_op jit(solution)/shard_map/while/body/eval_jaxpr/ppermute | solution.py:17
  350.7 13.6 %collective-permute-start = (bf16[2,64,3,64]{3,1,2,0:T(8,128)(2,1)S(1)}, bf16[2,64,3,64]{3,1,2,0:T(8,128)(2,1)S(1)}, u32[]{:S(2)}, u32[]{:S(2)}) collective-permute-start(bf16[2,64,3,64]{3,1,2,0:T(8,128)(2,1)S(1)} %copy.200), channel_id=1, source_target_pairs={{30,0},{0,2},{2,4},{4,6},{6,8},{8,10},{10,12},{12,14},{14,16},{16,... | collective-permute-start | bytes 147464 | tf_op jit(solution)/shard_map/while/body/eval_jaxpr/ppermute | solution.py:17
  350.7 13.5 %collective-permute-start.1 = (bf16[2,64,3,64]{3,1,2,0:T(8,128)(2,1)S(1)}, bf16[2,64,3,64]{3,1,2,0:T(8,128)(2,1)S(1)}, u32[]{:S(2)}, u32[]{:S(2)}) collective-permute-start(bf16[2,64,3,64]{3,1,2,0:T(8,128)(2,1)S(1)} %copy.201), channel_id=1, source_target_pairs={{30,0},{0,2},{2,4},{4,6},{6,8},{8,10},{10,12},{12,14},{14,16},{16,... | collective-permute-start | bytes 147464 | tf_op jit(solution)/shard_map/while/body/eval_jaxpr/ppermute | solution.py:17
  364.3 14.1 %collective-permute-start = (bf16[2,64,3,64]{3,1,2,0:T(8,128)(2,1)S(1)}, bf16[2,64,3,64]{3,1,2,0:T(8,128)(2,1)S(1)}, u32[]{:S(2)}, u32[]{:S(2)}) collective-permute-start(bf16[2,64,3,64]{3,1,2,0:T(8,128)(2,1)S(1)} %copy.200), channel_id=1, source_target_pairs={{30,0},{0,2},{2,4},{4,6},{6,8},{8,10},{10,12},{12,14},{14,16},{16,... | collective-permute-start | bytes 147464 | tf_op jit(solution)/shard_map/while/body/eval_jaxpr/ppermute | solution.py:17
  364.3 14.1 %collective-permute-start.1 = (bf16[2,64,3,64]{3,1,2,0:T(8,128)(2,1)S(1)}, bf16[2,64,3,64]{3,1,2,0:T(8,128)(2,1)S(1)}, u32[]{:S(2)}, u32[]{:S(2)}) collective-permute-start(bf16[2,64,3,64]{3,1,2,0:T(8,128)(2,1)S(1)} %copy.201), channel_id=1, source_target_pairs={{30,0},{0,2},{2,4},{4,6},{6,8},{8,10},{10,12},{12,14},{14,16},{16,... | collective-permute-start | bytes 147464 | tf_op jit(solution)/shard_map/while/body/eval_jaxpr/ppermute | solution.py:17
  378.4 16.3 %collective-permute-start = (bf16[2,64,3,64]{3,1,2,0:T(8,128)(2,1)S(1)}, bf16[2,64,3,64]{3,1,2,0:T(8,128)(2,1)S(1)}, u32[]{:S(2)}, u32[]{:S(2)}) collective-permute-start(bf16[2,64,3,64]{3,1,2,0:T(8,128)(2,1)S(1)} %copy.200), channel_id=1, source_target_pairs={{30,0},{0,2},{2,4},{4,6},{6,8},{8,10},{10,12},{12,14},{14,16},{16,... | collective-permute-start | bytes 147464 | tf_op jit(solution)/shard_map/while/body/eval_jaxpr/ppermute | solution.py:17
  378.9 15.9 %collective-permute-start.1 = (bf16[2,64,3,64]{3,1,2,0:T(8,128)(2,1)S(1)}, bf16[2,64,3,64]{3,1,2,0:T(8,128)(2,1)S(1)}, u32[]{:S(2)}, u32[]{:S(2)}) collective-permute-start(bf16[2,64,3,64]{3,1,2,0:T(8,128)(2,1)S(1)} %copy.201), channel_id=1, source_target_pairs={{30,0},{0,2},{2,4},{4,6},{6,8},{8,10},{10,12},{12,14},{14,16},{16,... | collective-permute-start | bytes 147464 | tf_op jit(solution)/shard_map/while/body/eval_jaxpr/ppermute | solution.py:17
  394.8 16.6 %collective-permute-start = (bf16[2,64,3,64]{3,1,2,0:T(8,128)(2,1)S(1)}, bf16[2,64,3,64]{3,1,2,0:T(8,128)(2,1)S(1)}, u32[]{:S(2)}, u32[]{:S(2)}) collective-permute-start(bf16[2,64,3,64]{3,1,2,0:T(8,128)(2,1)S(1)} %copy.200), channel_id=1, source_target_pairs={{30,0},{0,2},{2,4},{4,6},{6,8},{8,10},{10,12},{12,14},{14,16},{16,... | collective-permute-start | bytes 147464 | tf_op jit(solution)/shard_map/while/body/eval_jaxpr/ppermute | solution.py:17
  394.9 16.5 %collective-permute-start.1 = (bf16[2,64,3,64]{3,1,2,0:T(8,128)(2,1)S(1)}, bf16[2,64,3,64]{3,1,2,0:T(8,128)(2,1)S(1)}, u32[]{:S(2)}, u32[]{:S(2)}) collective-permute-start(bf16[2,64,3,64]{3,1,2,0:T(8,128)(2,1)S(1)} %copy.201), channel_id=1, source_target_pairs={{30,0},{0,2},{2,4},{4,6},{6,8},{8,10},{10,12},{12,14},{14,16},{16,... | collective-permute-start | bytes 147464 | tf_op jit(solution)/shard_map/while/body/eval_jaxpr/ppermute | solution.py:17
  411.4 14.1 %collective-permute-start = (bf16[2,64,3,64]{3,1,2,0:T(8,128)(2,1)S(1)}, bf16[2,64,3,64]{3,1,2,0:T(8,128)(2,1)S(1)}, u32[]{:S(2)}, u32[]{:S(2)}) collective-permute-start(bf16[2,64,3,64]{3,1,2,0:T(8,128)(2,1)S(1)} %copy.200), channel_id=1, source_target_pairs={{30,0},{0,2},{2,4},{4,6},{6,8},{8,10},{10,12},{12,14},{14,16},{16,... | collective-permute-start | bytes 147464 | tf_op jit(solution)/shard_map/while/body/eval_jaxpr/ppermute | solution.py:17
  411.5 14.0 %collective-permute-start.1 = (bf16[2,64,3,64]{3,1,2,0:T(8,128)(2,1)S(1)}, bf16[2,64,3,64]{3,1,2,0:T(8,128)(2,1)S(1)}, u32[]{:S(2)}, u32[]{:S(2)}) collective-permute-start(bf16[2,64,3,64]{3,1,2,0:T(8,128)(2,1)S(1)} %copy.201), channel_id=1, source_target_pairs={{30,0},{0,2},{2,4},{4,6},{6,8},{8,10},{10,12},{12,14},{14,16},{16,... | collective-permute-start | bytes 147464 | tf_op jit(solution)/shard_map/while/body/eval_jaxpr/ppermute | solution.py:17
  449.3 15.3 %reduce-scatter.10.cloned.1.call-start = ((), (), s32[]{:S(2)}) async-start(), calls=%async_computation.11 | async-start | bytes 442368 | tf_op jit(solution)/shard_map/reduce_scatter | solution.py:319
  450.7 25.4 %reduce-scatter.14.cloned.1.call-start = ((), (), s32[]{:S(2)}) async-start(), calls=%async_computation.13 | async-start | bytes 1105920 | tf_op jit(solution)/shard_map/reduce_scatter | solution.py:325
  452.0 36.3 %reduce-scatter.8.cloned.1.call-start = ((), (), s32[]{:S(2)}) async-start(), calls=%async_computation.10 | async-start | bytes 1105920 | tf_op jit(solution)/shard_map/reduce_scatter | solution.py:316
  454.5 47.1 %reduce-scatter.18.cloned.1.call-start = ((), (), s32[]{:S(2)}) async-start(), calls=%async_computation.15 | async-start | bytes 2654208 | tf_op jit(solution)/shard_map/reduce_scatter | solution.py:334
  456.7 58.4 %reduce-scatter.16.cloned.1.call-start = ((), (), s32[]{:S(2)}) async-start(), calls=%async_computation.14 | async-start | bytes 2654208 | tf_op jit(solution)/shard_map/reduce_scatter | solution.py:331
  458.6 69.7 %reduce-scatter.20.cloned.1.call-start = ((), (), s32[]{:S(2)}) async-start(), calls=%async_computation.16 | async-start | bytes 2654208 | tf_op jit(solution)/shard_map/reduce_scatter | solution.py:337
  460.5 238.8 %all-reduce.10.cloned.1.call-start = ((), (), s32[]{:S(2)}) async-start(), calls=%async_computation.17 | async-start | bytes 7372800 | tf_op jit(solution)/shard_map/psum | solution.py:345
  (130 other events, 1666.9 us)
Sparse Core Ops, SparseCore 0:
  9.6 12.7 all-gather.3
  24.0 11.2 all-gather.5
  36.8 11.2 all-gather.7
  449.4 4.1 reduce-scatter.11
  455.7 8.8 reduce-scatter.9
  466.7 9.3 reduce-scatter.13
  479.0 9.3 reduce-scatter.7
  491.2 10.4 reduce-scatter.17
  504.6 10.4 reduce-scatter.15
  517.8 10.4 reduce-scatter.19
  535.8 163.4 all-reduce.9
